TPU v7x, 128 devices: a whole 4x4x4 slice. The times are simulated.
128 devices in a mesh: grp: 8 (over x, core), loc: 16 (over z, y).
Axes of the slice: x: 4, y: 4, z: 4, core: 2. Of those that a mesh axis runs over, the one named last changes fastest.
Arguments:
- tokens: bfloat16 [16384, 2048], P(('grp', 'loc')), may hold values from -6 to 6
- expert_ids: int32 [16384, 2], P(('grp', 'loc')), may hold values from 0 to 127, all different within a row; in each aligned block of 128 rows (0 to 127, 128 to 255, ...) at most 4 rows name the same one
- gate_fixed: int32 [16384, 2], P(('grp', 'loc')), may hold values from 1 to 4096
- gate_weight: bfloat16 [128, 2048, 1024], P(('grp', 'loc')), may hold values from -0.125 to 0.125
- up_weight: bfloat16 [128, 2048, 1024], P(('grp', 'loc')), may hold values from -0.125 to 0.125
- down_weight: bfloat16 [128, 1024, 2048], P(('grp', 'loc')), may hold values from -0.1875 to 0.1875
Outputs:
- mixed: bfloat16 [16384, 2048], P(('grp', 'loc'))
Inputs may be any that keep to these rules, and one draw needn't show every extreme that they name: `expert_ids`: each row names two different experts; among the rows of one device no expert is named more than 4 times, and one is named exactly 4 times.
All inputs are finite; a program needn't handle non-finite values.
Results may differ from a plain program's by a relative error of at most 0.0058.
Values may be sent and summed in bfloat16 or wider, within the bound.
A program may use at most 64 MiB of HBM per device.

v0:
```python
import jax
import jax.numpy as jnp
from jax import lax
from jax.sharding import PartitionSpec as P


def expert_rows(rows, w_gate, w_up, w_down):
    gate = jnp.dot(rows, w_gate, preferred_element_type=jnp.float32)
    upper = jnp.dot(rows, w_up, preferred_element_type=jnp.float32)
    hidden = (jax.nn.silu(gate) * upper).astype(jnp.bfloat16)
    return jnp.dot(hidden, w_down, preferred_element_type=jnp.float32).astype(jnp.bfloat16)


def body(tokens, expert_ids, gate_fixed, gate_weight, up_weight, down_weight):
    n_grp = lax.axis_size("grp")
    n_loc = lax.axis_size("loc")
    devices = n_grp * n_loc
    rows = tokens.shape[0]
    width = tokens.shape[1]
    capacity = max(2, 4 * rows // devices)
    w_gate = gate_weight[0]
    w_up = up_weight[0]
    w_down = down_weight[0]
    flat_ids = expert_ids.reshape(-1)
    onehot = (flat_ids[:, None] == jnp.arange(devices, dtype=jnp.int32)[None, :]).astype(jnp.int32)
    before = jnp.cumsum(onehot, axis=0) - onehot
    slot = jnp.sum(before * onehot, axis=1)
    target = flat_ids * capacity + slot
    source = jnp.repeat(tokens, 2, axis=0)
    outgoing = jnp.zeros((devices * capacity, width), jnp.bfloat16).at[target].set(source)
    outgoing = outgoing.reshape(devices, capacity, width)
    arrived = lax.all_to_all(outgoing, ("grp", "loc"), split_axis=0, concat_axis=0, tiled=True)
    many = arrived.shape[1]
    result = expert_rows(arrived.reshape(devices * many, width), w_gate, w_up, w_down)
    result = result.reshape(devices, many, width)
    returned = lax.all_to_all(result, ("grp", "loc"), split_axis=0, concat_axis=0, tiled=True)
    back = returned.reshape(devices * capacity, width)[target]
    back = back.astype(jnp.float32).reshape(rows, 2, width)
    fixed = gate_fixed.astype(jnp.float32)
    weights = fixed / jnp.sum(fixed, axis=1, keepdims=True)
    mixed = jnp.sum(back * weights[:, :, None], axis=1)
    return mixed.astype(jnp.bfloat16)


def solution(mesh):
    placed = (
        P(("grp", "loc"), None),
        P(("grp", "loc"), None),
        P(("grp", "loc"), None),
        P(("grp", "loc"), None, None),
        P(("grp", "loc"), None, None),
        P(("grp", "loc"), None, None),
    )
    return jax.shard_map(
        body, mesh=mesh, in_specs=placed, out_specs=P(("grp", "loc"), None), check_vma=False
    )
```

profile of v0, /device:TPU:1, one launch (start us, length us, event | category | flops | bytes accessed | tf_op | source)
XLA Modules:
  0.0 117.8 jit_solution(14135791676908682873)
XLA Ops:
  0.0 0.8 copy.9
  0.8 0.1 eq.29
  0.9 0.1 eq.25
  1.1 0.7 broadcast_multiply_fusion
  1.8 0.1 copy.11
  1.9 0.2 fusion.15
  2.2 0.1 copy.8
  2.3 0.1 mul.36
  2.4 1.7 %broadcast_in_dim.5 = bf16[128,2,2048]{2,1,0:T(2,128)(2,1)S(1)} broadcast(bf16[128,2048]{1,0:T(8,128)(2,1)} %param.6), dimensions={0,2} | broadcast | bytes 1572864 | tf_op jit(solution)/shard_map/broadcast_in_dim | solution.py:29
  4.1 0.4 reshape.86
  4.5 0.2 fusion.17
  4.7 2.8 %scatter_custom_fusion = bf16[512,2048]{1,0:T(8,128)(2,1)S(1)} fusion(s32[256]{0:T(256)S(1)} %bitcast.36, bf16[256,2048]{1,0:T(8,128)(2,1)S(1)} %reshape.86, bf16[]{:T(256)} %constant.6.clone.1), kind=kCustom, calls=%fused_computation.11 | custom fusion | bytes 2097154 | tf_op jit(solution)/shard_map/scatter | solution.py:30
  7.6 2.2 %reshape.69 = bf16[128,4,2048]{2,1,0:T(4,128)(2,1)} reshape(bf16[512,2048]{1,0:T(8,128)(2,1)S(1)} %scatter_custom_fusion) | data formatting | bytes 4194304 | tf_op jit(solution)/shard_map/reshape | solution.py:31
  9.8 40.8 %all_to_all.10 = bf16[128,4,2048]{2,1,0:T(4,128)(2,1)S(1)} all-to-all(bf16[128,4,2048]{2,1,0:T(4,128)(2,1)} %reshape.69), channel_id=1, replica_groups=mesh['grp'=8,'loc'=16] {'grp','loc'}, dimensions={0} | all-to-all | bytes 4194304 | tf_op jit(solution)/shard_map/all_to_all | solution.py:32
  50.6 2.0 %reshape.70 = bf16[512,2048]{1,0:T(8,128)(2,1)} reshape(bf16[128,4,2048]{2,1,0:T(4,128)(2,1)S(1)} %all_to_all.10) | data formatting | bytes 4194304 | tf_op jit(solution)/shard_map/reshape | solution.py:34
  52.6 0.0 copy-start
  52.6 6.6 %fusion.4 = f32[512,1024]{1,0:T(8,128)} fusion(bf16[512,2048]{1,0:T(8,128)(2,1)} %reshape.70, bf16[1,2048,1024]{2,1,0:T(8,128)(2,1)} %param.9), kind=kOutput, calls=%fused_computation.6 | convolution fusion | flops 2147483648 | bytes 8388608 | tf_op jit(solution)/shard_map/dot_general | solution.py:8
  59.3 0.0 copy-done
  59.3 9.9 %fusion.6 = bf16[512,2048]{1,0:T(8,128)(2,1)} fusion(bf16[1,1024,2048]{2,1,0:T(8,128)(2,1)} %param.11, f32[512,1024]{1,0:T(8,128)} %fusion.4, bf16[512,2048]{1,0:T(8,128)(2,1)S(1)} %copy-done, bf16[1,2048,1024]{2,1,0:T(8,128)(2,1)} %param.10), kind=kOutput, calls=%fused_computation.8 | convolution fusion | flops 4299161600 | bytes 14680064 | tf_op jit(solution)/shard_map/dot_general | solution.py:11
  69.2 4.1 %reshape.71 = bf16[128,4,2048]{2,1,0:T(4,128)(2,1)} reshape(bf16[512,2048]{1,0:T(8,128)(2,1)} %fusion.6) | data formatting | bytes 4194304 | tf_op jit(solution)/shard_map/reshape | solution.py:35
  73.3 0.0 copy-start.1
  73.3 6.2 %all-to-all-start.1 = ((bf16[128,4,2048]{2,1,0:T(4,128)(2,1)}), bf16[128,4,2048]{2,1,0:T(4,128)(2,1)}, u32[]{:S(2)}, u32[]{:S(2)}) async-start(bf16[128,4,2048]{2,1,0:T(4,128)(2,1)} %reshape.71), calls=%async_computation.1 | async-start | bytes 4194304 | tf_op jit(solution)/shard_map/all_to_all | solution.py:36
  79.5 0.0 copy-done.1
  79.5 0.1 copy.13
  79.6 28.9 %all-to-all-done.1 = bf16[128,4,2048]{2,1,0:T(4,128)(2,1)} async-done(((bf16[128,4,2048]{2,1,0:T(4,128)(2,1)}), bf16[128,4,2048]{2,1,0:T(4,128)(2,1)}, u32[]{:S(2)}, u32[]{:S(2)}) %all-to-all-start.1) | async-done | bytes 2097184 | tf_op jit(solution)/shard_map/all_to_all | solution.py:36
  108.5 2.5 %reshape.72 = bf16[512,2048]{1,0:T(8,128)(2,1)S(1)} reshape(bf16[128,4,2048]{2,1,0:T(4,128)(2,1)} %all-to-all-done.1) | data formatting | bytes 4194304 | tf_op jit(solution)/shard_map/reshape | solution.py:37
  111.0 1.4 %gather_fusion = bf16[256,2048]{1,0:T(8,128)(2,1)S(1)} fusion(bf16[512,2048]{1,0:T(8,128)(2,1)S(1)} %reshape.72, s32[1024]{0:T(1024)S(1)} %pad_clamp_fusion), kind=kCustom, calls=%fused_computation | custom fusion | bytes 2098176 | tf_op jit(solution)/shard_map/gather | solution.py:37
  112.4 1.3 %reshape.73 = f32[128,2,2048]{2,1,0:T(2,128)S(1)} reshape(bf16[256,2048]{1,0:T(8,128)(2,1)S(1)} %gather_fusion) | data formatting | bytes 3145728 | tf_op jit(solution)/shard_map/convert_element_type | solution.py:38
  113.8 4.0 %multiply_reduce_fusion = bf16[128,2048]{1,0:T(8,128)(2,1)} fusion(f32[128,2,2048]{2,1,0:T(2,128)S(1)} %reshape.73, f32[128,2]{1,0:T(8,128)S(1)} %copy.13), kind=kLoop, calls=%fused_computation.9 | loop fusion | flops 786432 | bytes 2622464 | tf_op jit(solution)/shard_map/reduce_sum | solution.py:41
  (10 shorter events, 0.1 us)
Async XLA Ops:
  52.6 6.7 %copy-start = (bf16[512,2048]{1,0:T(8,128)(2,1)S(1)}, bf16[512,2048]{1,0:T(8,128)(2,1)}, u32[]{:S(2)}) copy-start(bf16[512,2048]{1,0:T(8,128)(2,1)} %reshape.70) | copy-start | bytes 6291460
  73.3 6.2 %copy-start.1 = (s32[128,2]{0,1:T(2,128)S(1)}, s32[128,2]{0,1:T(2,128)}, u32[]{:S(2)}) copy-start(s32[128,2]{0,1:T(2,128)} %param.8) | copy-start | bytes 3076
  73.3 35.2 %all-to-all-start.1 = ((bf16[128,4,2048]{2,1,0:T(4,128)(2,1)}), bf16[128,4,2048]{2,1,0:T(4,128)(2,1)}, u32[]{:S(2)}, u32[]{:S(2)}) async-start(bf16[128,4,2048]{2,1,0:T(4,128)(2,1)} %reshape.71), calls=%async_computation.1 | async-start | bytes 4194304 | tf_op jit(solution)/shard_map/all_to_all | solution.py:36
where the time goes:
time: 118 us
  blocking collectives  40.8 us (35%)
  waiting for transfers between devices  28.9 us (24%)
  local copies, waits for them, and re-layouts  20.1 us (17%)
  matrix products  16.6 us (14%)
  starting transfers between devices  6.15 us (5%)
  other arithmetic  5.19 us (4%)
    all_to_all x1, blocking collectives, body(): lax.all_to_all(outgoing, ('grp', 'loc'), split_axis=0, concat_axis=0, til...  40.8 us
    all_to_all x1, waiting for transfers between devices, body(): lax.all_to_all(result, ('grp', 'loc'), split_axis=0, concat_axis=0, tiled...  28.9 us
    dot_general x1, matrix products, expert_rows(): jnp.dot(hidden, w_down, preferred_element_type=jnp.float32)  9.94 us
    dot_general x1, matrix products, expert_rows(): gate = jnp.dot(rows, w_gate, preferred_element_type=jnp.float32)  6.65 us
    all_to_all x1, starting transfers between devices, body(): lax.all_to_all(result, ('grp', 'loc'), split_axis=0, concat_axis=0, tiled...  6.15 us
    reshape x1, local copies, waits for them, and re-layouts, body(): result = result.reshape(devices, many, width)  4.11 us
    reduce_sum x1, other arithmetic, body(): mixed = jnp.sum(back * weights[:, :, None], axis=1)  4.03 us
    scatter x1, local copies, waits for them, and re-layouts, body(): jnp.zeros((devices * capacity, width), jnp.bfloat16).at[target].set(source)  2.82 us
  transfers between devices with their start and end apart: 1, of which 1 were waited for; matrix products, arithmetic and copies ran while one was open for 0% of the time, Pallas kernels for 0%

commit v1 on v0

v1 whole, which is shorter than its diff:
```python
import functools

import jax
import jax.numpy as jnp
import numpy as np
from jax import lax
from jax.experimental import pallas as pl
from jax.experimental.pallas import tpu as pltpu
from jax.sharding import PartitionSpec as P

MESH = pl.DeviceIdType.MESH
CAP = 4
CHUNKS = 4


def far(offset):
    return sum(min(step, 4 - step) for step in (offset[0], offset[2], offset[3]))


OFFSETS = sorted(
    ((dx, dc, dz, dy) for dx in range(4) for dc in range(2) for dz in range(4) for dy in range(4) if dx + dc + dz + dy),
    key=lambda offset: -far(offset),
) + [(0, 0, 0, 0)]
N = len(OFFSETS)
PER = N // CHUNKS
ROWS = PER * CAP


def place():
    grp, loc = lax.axis_index("grp"), lax.axis_index("loc")
    return grp // 2, grp % 2, loc // 4, loc % 4


def device_at(offset, sign):
    x, c, z, y = place()
    dx, dc, dz, dy = offset
    return (
        (x + sign * dx + 4) % 4 * 2 + (c + dc) % 2,
        (z + sign * dz + 4) % 4 * 4 + (y + sign * dy + 4) % 4,
    )


def kernel(
    tokens, ids, gates, table, w_gate, w_up, w_down, out,
    gate_v, up_v, down_v, send, recv, ret, back, mix, total,
    weight_sem, send_sem, recv_sem, ret_sem, back_sem, own_sem,
):
    barrier = pltpu.get_barrier_semaphore()
    for offset in OFFSETS[:-1]:
        pl.semaphore_signal(barrier, 1, device_id=device_at(offset, 1), device_id_type=MESH)
    loads = [
        pltpu.make_async_copy(src.at[0], dst, weight_sem.at[i])
        for i, (src, dst) in enumerate(((w_gate, gate_v), (w_up, up_v), (w_down, down_v)))
    ]
    for load in loads:
        load.start()

    x, c, z, y = place()
    expert = ((x + table[0:1, :]) % 4 * 2 + (c + table[1:2, :]) % 2) * 16
    expert = expert + (z + table[2:3, :]) % 4 * 4 + (y + table[3:4, :]) % 4
    first = ids[:, 0:1] == expert
    second = ids[:, 1:2] == expert
    named = first | second
    rows = tokens.shape[0]
    lower = lax.broadcasted_iota(jnp.int32, (rows, rows), 0) > lax.broadcasted_iota(jnp.int32, (rows, rows), 1)
    before = jnp.dot(
        lower.astype(jnp.bfloat16), named.astype(jnp.bfloat16), preferred_element_type=jnp.float32
    )
    chosen = named & (before == table[4:5, :].astype(jnp.float32))
    fixed = gates[...].astype(jnp.float32)
    weights = fixed / jnp.sum(fixed, axis=1, keepdims=True)
    scale = jnp.where(chosen, jnp.where(first, weights[:, 0:1], weights[:, 1:2]), 0.0)
    mix[0] = scale.astype(jnp.bfloat16)
    mix[1] = (scale - mix[0].astype(jnp.float32)).astype(jnp.bfloat16)
    pick = jnp.where(chosen, 1.0, 0.0).astype(jnp.bfloat16)
    for k in range(CHUNKS):
        part = lax.dot_general(
            pick[:, k * ROWS : (k + 1) * ROWS], tokens[...], (((0,), (0,)), ((), ())), preferred_element_type=jnp.float32
        )
        send[k * PER : (k + 1) * PER] = part.astype(jnp.bfloat16).reshape(PER, CAP, -1)

    pl.semaphore_wait(barrier, N - 1)
    own = pltpu.make_async_copy(send.at[N - 1], recv.at[N - 1], own_sem.at[0])
    for i, offset in enumerate(OFFSETS[:-1]):
        pltpu.make_async_remote_copy(
            send.at[i], recv.at[i], send_sem, recv_sem.at[i // PER],
            device_id=device_at(offset, 1), device_id_type=MESH,
        ).start()
    own.start()
    for load in loads:
        load.wait()

    def arrived(buffer, sem, k):
        count = PER - (k == CHUNKS - 1)
        landed = buffer.at[pl.ds(k * PER, count)]
        pltpu.make_async_copy(landed, landed, sem.at[k]).wait()

    for k in range(CHUNKS):
        arrived(recv, recv_sem, k)
        if k == CHUNKS - 1:
            own.wait()
        block = recv[k * PER : (k + 1) * PER].reshape(ROWS, -1)
        gate = jnp.dot(block, gate_v[...], preferred_element_type=jnp.float32)
        upper = jnp.dot(block, up_v[...], preferred_element_type=jnp.float32)
        hidden = (gate / (1.0 + jnp.exp(-gate)) * upper).astype(jnp.bfloat16)
        result = jnp.dot(hidden, down_v[...], preferred_element_type=jnp.float32)
        ret[k * PER : (k + 1) * PER] = result.astype(jnp.bfloat16).reshape(PER, CAP, -1)
        for i in range(k * PER, min((k + 1) * PER, N - 1)):
            pltpu.make_async_remote_copy(
                ret.at[i], back.at[i], ret_sem, back_sem.at[k],
                device_id=device_at(OFFSETS[i], -1), device_id_type=MESH,
            ).start()
    home = pltpu.make_async_copy(ret.at[N - 1], back.at[N - 1], own_sem.at[1])
    home.start()

    for k in range(CHUNKS):
        arrived(back, back_sem, k)
        if k == CHUNKS - 1:
            home.wait()
        block = back[k * PER : (k + 1) * PER].reshape(ROWS, -1)
        columns = slice(k * ROWS, (k + 1) * ROWS)
        part = jnp.dot(mix[0, :, columns], block, preferred_element_type=jnp.float32)
        part = part + jnp.dot(mix[1, :, columns], block, preferred_element_type=jnp.float32)
        total[...] = part if k == 0 else total[...] + part
    out[...] = total[...].astype(out.dtype)
    sent = send.at[pl.ds(0, N - 1)]
    pltpu.make_async_copy(sent, sent, send_sem).wait()
    pltpu.make_async_copy(sent, sent, ret_sem).wait()


def body(tokens, expert_ids, gate_fixed, gate_weight, up_weight, down_weight):
    rows, width = tokens.shape
    hidden = gate_weight.shape[2]
    table = np.zeros((8, N * CAP), np.int32)
    for i, offset in enumerate(OFFSETS):
        for j in range(CAP):
            table[:4, i * CAP + j] = offset
            table[4, i * CAP + j] = j
    vmem = pl.BlockSpec(memory_space=pltpu.VMEM)
    hbm = pl.BlockSpec(memory_space=pl.ANY)
    slots = pltpu.VMEM((N, CAP, width), jnp.bfloat16)
    dma = pltpu.SemaphoreType.DMA
    return pl.pallas_call(
        kernel,
        out_shape=jax.ShapeDtypeStruct((rows, width), jnp.bfloat16),
        in_specs=[vmem] * 4 + [hbm] * 3,
        out_specs=vmem,
        scratch_shapes=[
            pltpu.VMEM((width, hidden), jnp.bfloat16),
            pltpu.VMEM((width, hidden), jnp.bfloat16),
            pltpu.VMEM((hidden, width), jnp.bfloat16),
            slots, slots, slots, slots,
            pltpu.VMEM((2, rows, N * CAP), jnp.bfloat16),
            pltpu.VMEM((rows, width), jnp.float32),
            dma((3,)), dma, dma((CHUNKS,)), dma, dma((CHUNKS,)), dma((2,)),
        ],
        compiler_params=pltpu.CompilerParams(
            collective_id=0, has_side_effects=True, vmem_limit_bytes=56 << 20
        ),
    )(tokens, expert_ids, gate_fixed, jnp.asarray(table), gate_weight, up_weight, down_weight)


def solution(mesh):
    rows = P(("grp", "loc"), None)
    experts = P(("grp", "loc"), None, None)
    return jax.shard_map(
        body, mesh=mesh, in_specs=(rows, rows, rows, experts, experts, experts), out_specs=rows, check_vma=False
    )
```

time: 118 us -> 65.7 us (0.56)
  Pallas kernels: 0 us -> 60.8 us
  blocking collectives: 40.8 us -> 0 us
  waiting for transfers between devices: 28.9 us -> 0 us
  matrix products: 16.6 us -> 0 us
  local copies, waits for them, and re-layouts: 20.1 us -> 4.7 us
  starting transfers between devices: 6.15 us -> 0 us
  other arithmetic: 5.19 us -> 0 us
    pallas_call x0 -> x1, Pallas kernels: none -> 60.8 us  [body(): pl.pallas_call(kernel, out_shape=jax.ShapeDtypeStruct((rows, width), jnp....]
    all_to_all x1 -> x0, blocking collectives: 40.8 us -> none  [body(): lax.all_to_all(outgoing, ('grp', 'loc'), split_axis=0, concat_axis=0, til...]
    all_to_all x1 -> x0, waiting for transfers between devices: 28.9 us -> none  [body(): lax.all_to_all(result, ('grp', 'loc'), split_axis=0, concat_axis=0, tiled...]
    dot_general x2 -> x0, matrix products: 16.6 us -> none  [the longest x1 9.94 us: expert_rows(): jnp.dot(hidden, w_down, preferred_element_type=jnp.float32)]
    reshape x5 -> x0, local copies, waits for them, and re-layouts: 11.4 us -> none  [the longest x1 4.11 us: body(): result = result.reshape(devices, many, width)]
    all_to_all x1 -> x0, starting transfers between devices: 6.15 us -> none  [body(): lax.all_to_all(result, ('grp', 'loc'), split_axis=0, concat_axis=0, tiled...]
    reduce_sum x3 -> x0, other arithmetic: 4.23 us -> none  [the longest x1 4.03 us: body(): mixed = jnp.sum(back * weights[:, :, None], axis=1)]
    unnamed x6 -> x3, local copies, waits for them, and re-layouts: 0.8 us -> 4.7 us
  transfers between devices with their start and end apart: 1 -> 0, of which waited for: 1 -> 0; matrix products, arithmetic and copies ran while one was open for 0% -> 0% of each run, Pallas kernels for 0% -> 0%
where the time goes in v1:
time: 65.7 us; the launch traced here: 65.5 us
  Pallas kernels  60.8 us (93%)
  local copies, waits for them, and re-layouts  4.7 us (7%)
    pallas_call x1, Pallas kernels, body(): pl.pallas_call(kernel, out_shape=jax.ShapeDtypeStruct((rows, width), jnp....  60.8 us
    unnamed x3, local copies, waits for them, and re-layouts  4.7 us

profile of v1, /device:TPU:1, one launch (start us, length us, event | category | flops | bytes accessed | tf_op | source)
XLA Modules:
  0.0 65.5 jit_solution(638908975818135096)
XLA Ops:
  0.0 1.4 %copy.8.ids = s32[128,2]{1,0:T(8,128)} copy(s32[128,2]{0,1:T(2,128)} %param.8) | data formatting | bytes 2048 | tf_op args[1]
  1.4 1.4 %copy.9.gates = s32[128,2]{1,0:T(8,128)} copy(s32[128,2]{0,1:T(2,128)} %param.9) | data formatting | bytes 2048 | tf_op args[2]
  2.8 60.8 %shard_map.73 = bf16[128,2048]{1,0:T(8,128)(2,1)} custom-call(bf16[128,2048]{1,0:T(8,128)(2,1)} %tokens.1, s32[128,2]{1,0:T(8,128)} %copy.8.ids, s32[128,2]{1,0:T(8,128)} %copy.9.gates, s32[8,512]{1,0:T(8,128)} %constant.2.clone.table, bf16[1,2048,1024]{2,1,0:T(8,128)(2,1)} %w_gate.1, bf16[1,2048,1024]{2,1,0:T(8,128)(2,1)} %w_up.1, bf16[1,1024,2048]{2,1,0:T(8,128)(2,1)} %w_down.1), custom_call_target="tpu_custom_call" | custom-call | tf_op jit(solution)/shard_map/pallas_call | solution.py:143
  63.7 1.9 %copy.11 = bf16[128,2048]{1,0:T(8,128)(2,1)} copy(bf16[128,2048]{1,0:T(8,128)(2,1)} %shard_map.73) | data formatting | bytes 1048576

commit v2 on v1

v2 whole, which is shorter than its diff:
```python
import functools

import jax
import jax.numpy as jnp
import numpy as np
from jax import lax
from jax.experimental import pallas as pl
from jax.experimental.pallas import tpu as pltpu
from jax.sharding import PartitionSpec as P

MESH = pl.DeviceIdType.MESH
CAP = 4
CHUNKS = 4


def far(offset):
    return sum(min(step, 4 - step) for step in (offset[0], offset[2], offset[3]))


OFFSETS = sorted(
    ((dx, dc, dz, dy) for dx in range(4) for dc in range(2) for dz in range(4) for dy in range(4) if dx + dc + dz + dy),
    key=lambda offset: -far(offset),
) + [(0, 0, 0, 0)]
N = len(OFFSETS)
PER = N // CHUNKS
ROWS = PER * CAP


def place():
    grp, loc = lax.axis_index("grp"), lax.axis_index("loc")
    return grp // 2, grp % 2, loc // 4, loc % 4


def device_at(offset, sign):
    x, c, z, y = place()
    dx, dc, dz, dy = offset
    return (
        (x + sign * dx + 4) % 4 * 2 + (c + dc) % 2,
        (z + sign * dz + 4) % 4 * 4 + (y + sign * dy + 4) % 4,
    )


def spread(index):
    return index % 4 + index // 4 % 4 * 8 + index // 16 % 2 * 64 + index // 32 * 256


def kernel(
    tokens, ids, gates, table, w_gate, w_up, w_down, out,
    tokens_v, ids_v, gates_v, table_v, gate_v, up_v, down_v, send, recv, ret, back, mix, total,
    load_sem, send_sem, recv_sem, ret_sem, back_sem, own_sem,
):
    barrier = pltpu.get_barrier_semaphore()
    for offset in OFFSETS[:-1]:
        pl.semaphore_signal(barrier, 1, device_id=device_at(offset, 1), device_id_type=MESH)
    loads = [
        pltpu.make_async_copy(src, dst, load_sem.at[i])
        for i, (src, dst) in enumerate((
            (ids, ids_v), (table, table_v), (gates, gates_v), (tokens, tokens_v),
            (w_gate.at[0], gate_v), (w_up.at[0], up_v), (w_down.at[0], down_v),
        ))
    ]
    for load in loads:
        load.start()

    x, c, z, y = place()
    for load in loads[:3]:
        load.wait()
    expert = (table_v[...] + spread(x * 32 + c * 16 + z * 4 + y)) & spread(N - 1)
    asked = spread(ids_v[...])
    first = asked[0:1, :] == expert
    second = asked[1:2, :] == expert
    named = first | second
    rows = tokens.shape[0]
    earlier = lax.broadcasted_iota(jnp.int32, (rows, rows), 0) < lax.broadcasted_iota(jnp.int32, (rows, rows), 1)
    before = jnp.dot(
        named.astype(jnp.bfloat16), earlier.astype(jnp.bfloat16), preferred_element_type=jnp.float32
    )
    slot = lax.broadcasted_iota(jnp.int32, named.shape, 0) % CAP
    chosen = named & (before == slot.astype(jnp.float32))
    pick = chosen.astype(jnp.bfloat16)
    loads[3].wait()
    for k in range(CHUNKS):
        part = jnp.dot(pick[k * ROWS : (k + 1) * ROWS], tokens_v[...], preferred_element_type=jnp.float32)
        send[k * PER : (k + 1) * PER] = part.astype(jnp.bfloat16).reshape(PER, CAP, -1)
        if k == 0:
            pl.semaphore_wait(barrier, N - 1)
        for i in range(k * PER, min((k + 1) * PER, N - 1)):
            pltpu.make_async_remote_copy(
                send.at[i], recv.at[i], send_sem, recv_sem.at[k],
                device_id=device_at(OFFSETS[i], 1), device_id_type=MESH,
            ).start()
    own = pltpu.make_async_copy(send.at[N - 1], recv.at[N - 1], own_sem.at[0])
    own.start()

    fixed = gates_v[...].astype(jnp.float32)
    weights = fixed / jnp.sum(fixed, axis=0, keepdims=True)
    scale = jnp.where(chosen, jnp.where(first, weights[0:1, :], weights[1:2, :]), 0.0).T
    mix[0] = scale.astype(jnp.bfloat16)
    mix[1] = (scale - mix[0].astype(jnp.float32)).astype(jnp.bfloat16)
    for load in loads[4:]:
        load.wait()

    def arrived(buffer, sem, k):
        count = PER - (k == CHUNKS - 1)
        landed = buffer.at[pl.ds(k * PER, count)]
        pltpu.make_async_copy(landed, landed, sem.at[k]).wait()

    for k in range(CHUNKS):
        arrived(recv, recv_sem, k)
        if k == CHUNKS - 1:
            own.wait()
        block = recv[k * PER : (k + 1) * PER].reshape(ROWS, -1)
        gate = jnp.dot(block, gate_v[...], preferred_element_type=jnp.float32)
        upper = jnp.dot(block, up_v[...], preferred_element_type=jnp.float32)
        hidden = (gate / (1.0 + jnp.exp(-gate)) * upper).astype(jnp.bfloat16)
        result = jnp.dot(hidden, down_v[...], preferred_element_type=jnp.float32)
        ret[k * PER : (k + 1) * PER] = result.astype(jnp.bfloat16).reshape(PER, CAP, -1)
        for i in range(k * PER, min((k + 1) * PER, N - 1)):
            pltpu.make_async_remote_copy(
                ret.at[i], back.at[i], ret_sem, back_sem.at[k],
                device_id=device_at(OFFSETS[i], -1), device_id_type=MESH,
            ).start()
    home = pltpu.make_async_copy(ret.at[N - 1], back.at[N - 1], own_sem.at[1])
    home.start()

    for k in range(CHUNKS):
        arrived(back, back_sem, k)
        if k == CHUNKS - 1:
            home.wait()
        block = back[k * PER : (k + 1) * PER].reshape(ROWS, -1)
        columns = slice(k * ROWS, (k + 1) * ROWS)
        part = jnp.dot(mix[0, :, columns], block, preferred_element_type=jnp.float32)
        part = part + jnp.dot(mix[1, :, columns], block, preferred_element_type=jnp.float32)
        if k == CHUNKS - 1:
            out[...] = (total[...] + part).astype(out.dtype)
        else:
            total[...] = part if k == 0 else total[...] + part
    sent = send.at[pl.ds(0, N - 1)]
    pltpu.make_async_copy(sent, sent, send_sem).wait()
    pltpu.make_async_copy(sent, sent, ret_sem).wait()


def body(tokens, expert_ids, gate_fixed, gate_weight, up_weight, down_weight):
    rows, width = tokens.shape
    hidden = gate_weight.shape[2]
    table = np.zeros((N * CAP, rows), np.int32)
    for i, (dx, dc, dz, dy) in enumerate(OFFSETS):
        table[i * CAP : (i + 1) * CAP] = spread(dx * 32 + dc * 16 + dz * 4 + dy)
    vmem = pl.BlockSpec(memory_space=pltpu.VMEM)
    hbm = pl.BlockSpec(memory_space=pl.ANY)
    slots = pltpu.VMEM((N, CAP, width), jnp.bfloat16)
    dma = pltpu.SemaphoreType.DMA
    return pl.pallas_call(
        kernel,
        out_shape=pltpu.VMEM((rows, width), jnp.bfloat16),
        in_specs=[hbm] * 7,
        out_specs=vmem,
        scratch_shapes=[
            pltpu.VMEM((rows, width), jnp.bfloat16),
            pltpu.VMEM((2, rows), jnp.int32),
            pltpu.VMEM((2, rows), jnp.int32),
            pltpu.VMEM((N * CAP, rows), jnp.int32),
            pltpu.VMEM((width, hidden), jnp.bfloat16),
            pltpu.VMEM((width, hidden), jnp.bfloat16),
            pltpu.VMEM((hidden, width), jnp.bfloat16),
            slots, slots, slots, slots,
            pltpu.VMEM((2, rows, N * CAP), jnp.bfloat16),
            pltpu.VMEM((rows, width), jnp.float32),
            dma((7,)), dma, dma((CHUNKS,)), dma, dma((CHUNKS,)), dma((2,)),
        ],
        compiler_params=pltpu.CompilerParams(
            collective_id=0, has_side_effects=True, vmem_limit_bytes=60 << 20
        ),
    )(tokens, expert_ids.T, gate_fixed.T, jnp.asarray(table), gate_weight, up_weight, down_weight)


def solution(mesh):
    rows = P(("grp", "loc"), None)
    experts = P(("grp", "loc"), None, None)
    return jax.shard_map(
        body, mesh=mesh, in_specs=(rows, rows, rows, experts, experts, experts), out_specs=rows, check_vma=False
    )
```

time: 65.7 us -> 61.4 us (0.935)
  local copies, waits for them, and re-layouts: 4.7 us -> 0.8 us
    unnamed x3 -> x1, local copies, waits for them, and re-layouts: 4.7 us -> 0.8 us
where the time goes in v2:
time: 61.4 us; the launch traced here: 61.3 us
  Pallas kernels  60.5 us (99%)
  local copies, waits for them, and re-layouts  0.8 us (1%)
    pallas_call x1, Pallas kernels, body(): pl.pallas_call(kernel, out_shape=pltpu.VMEM((rows, width), jnp.bfloat16),...  60.5 us

profile of v2, /device:TPU:1, one launch (start us, length us, event | category | flops | bytes accessed | tf_op | source)
XLA Modules:
  0.0 61.3 jit_solution(6272905026271123107)
XLA Ops:
  0.0 60.5 %shard_map.73 = bf16[128,2048]{1,0:T(8,128)(2,1)S(1)} custom-call(bf16[128,2048]{1,0:T(8,128)(2,1)} %tokens.1, s32[2,128]{1,0:T(2,128)} %bitcast.2, s32[2,128]{1,0:T(2,128)} %bitcast.3, s32[512,128]{1,0:T(8,128)} %constant.2.clone.table, bf16[1,2048,1024]{2,1,0:T(8,128)(2,1)} %w_gate.1, bf16[1,2048,1024]{2,1,0:T(8,128)(2,1)} %w_up.1, ...), custom_call_target="tpu_custom_call" | custom-call | tf_op jit(solution)/shard_map/pallas_call | solution.py:153
  60.5 0.8 %copy.9 = bf16[128,2048]{1,0:T(8,128)(2,1)} copy(bf16[128,2048]{1,0:T(8,128)(2,1)S(1)} %shard_map.73) | data formatting | bytes 1048576

commit v3 on v2

--- a/solution.py
+++ b/solution.py
@@ -17,11 +17,17 @@
     return sum(min(step, 4 - step) for step in (offset[0], offset[2], offset[3]))
 
 
+def turns(offset):
+    return (offset[0] + offset[1] > 0) + (offset[2] > 0) + (offset[3] > 0)
+
+
 OFFSETS = sorted(
     ((dx, dc, dz, dy) for dx in range(4) for dc in range(2) for dz in range(4) for dy in range(4) if dx + dc + dz + dy),
-    key=lambda offset: -far(offset),
+    key=lambda offset: (turns(offset) == 3, -far(offset)),
 ) + [(0, 0, 0, 0)]
 N = len(OFFSETS)
+NEAR = [offset for offset in OFFSETS[:-1] if turns(offset) < 3]
+COLUMN = [(0, 0, dz, 0) for dz in range(1, 4)]
 PER = N // CHUNKS
 ROWS = PER * CAP
 
@@ -47,10 +53,10 @@
 def kernel(
     tokens, ids, gates, table, w_gate, w_up, w_down, out,
     tokens_v, ids_v, gates_v, table_v, gate_v, up_v, down_v, send, recv, ret, back, mix, total,
-    load_sem, send_sem, recv_sem, ret_sem, back_sem, own_sem,
+    load_sem, send_sem, recv_sem, ret_sem, back_sem, own_sem, rest_sem,
 ):
     barrier = pltpu.get_barrier_semaphore()
-    for offset in OFFSETS[:-1]:
+    for offset in NEAR:
         pl.semaphore_signal(barrier, 1, device_id=device_at(offset, 1), device_id_type=MESH)
     loads = [
         pltpu.make_async_copy(src, dst, load_sem.at[i])
@@ -83,7 +89,11 @@
         part = jnp.dot(pick[k * ROWS : (k + 1) * ROWS], tokens_v[...], preferred_element_type=jnp.float32)
         send[k * PER : (k + 1) * PER] = part.astype(jnp.bfloat16).reshape(PER, CAP, -1)
         if k == 0:
-            pl.semaphore_wait(barrier, N - 1)
+            pl.semaphore_wait(barrier, len(NEAR))
+            for offset in COLUMN:
+                pl.semaphore_signal(rest_sem, 1, device_id=device_at(offset, 1), device_id_type=MESH)
+        if (k + 1) * PER > len(NEAR) >= k * PER:
+            pl.semaphore_wait(rest_sem, len(COLUMN))
         for i in range(k * PER, min((k + 1) * PER, N - 1)):
             pltpu.make_async_remote_copy(
                 send.at[i], recv.at[i], send_sem, recv_sem.at[k],
@@ -166,7 +176,7 @@
             slots, slots, slots, slots,
             pltpu.VMEM((2, rows, N * CAP), jnp.bfloat16),
             pltpu.VMEM((rows, width), jnp.float32),
-            dma((7,)), dma, dma((CHUNKS,)), dma, dma((CHUNKS,)), dma((2,)),
+            dma((7,)), dma, dma((CHUNKS,)), dma, dma((CHUNKS,)), dma((2,)), pltpu.SemaphoreType.REGULAR,
         ],
         compiler_params=pltpu.CompilerParams(
             collective_id=0, has_side_effects=True, vmem_limit_bytes=60 << 20

time: 61.4 us -> 59.7 us (0.972)
  Pallas kernels: 60.5 us -> 58.8 us
    pallas_call x1, Pallas kernels: 60.5 us -> 58.8 us  [body(): pl.pallas_call(kernel, out_shape=pltpu.VMEM((rows, width), jnp.bfloat16),...]
where the time goes in v3:
time: 59.7 us; the launch traced here: 59.6 us
  Pallas kernels  58.8 us (98%)
  local copies, waits for them, and re-layouts  0.8 us (1%)
    pallas_call x1, Pallas kernels, body(): pl.pallas_call(kernel, out_shape=pltpu.VMEM((rows, width), jnp.bfloat16),...  58.8 us

profile of v3, /device:TPU:1, one launch (start us, length us, event | category | flops | bytes accessed | tf_op | source)
XLA Modules:
  0.0 59.6 jit_solution(5939535088726043659)
XLA Ops:
  0.0 58.8 %shard_map.73 = bf16[128,2048]{1,0:T(8,128)(2,1)S(1)} custom-call(bf16[128,2048]{1,0:T(8,128)(2,1)} %tokens.1, s32[2,128]{1,0:T(2,128)} %bitcast.2, s32[2,128]{1,0:T(2,128)} %bitcast.3, s32[512,128]{1,0:T(8,128)} %constant.2.clone.table, bf16[1,2048,1024]{2,1,0:T(8,128)(2,1)} %w_gate.1, bf16[1,2048,1024]{2,1,0:T(8,128)(2,1)} %w_up.1, ...), custom_call_target="tpu_custom_call" | custom-call | tf_op jit(solution)/shard_map/pallas_call | solution.py:163
  58.8 0.8 %copy.9 = bf16[128,2048]{1,0:T(8,128)(2,1)} copy(bf16[128,2048]{1,0:T(8,128)(2,1)S(1)} %shard_map.73) | data formatting | bytes 1048576

commit v4 on v3

--- a/solution.py
+++ b/solution.py
@@ -40,10 +40,9 @@
 def device_at(offset, sign):
     x, c, z, y = place()
     dx, dc, dz, dy = offset
-    return (
-        (x + sign * dx + 4) % 4 * 2 + (c + dc) % 2,
-        (z + sign * dz + 4) % 4 * 4 + (y + sign * dy + 4) % 4,
-    )
+    core = (c + dc) % 2
+    way = 1 - 2 * c if sign > 0 else 2 * core - 1
+    return (x + way * dx + 4) % 4 * 2 + core, (z + way * dz + 4) % 4 * 4 + (y + way * dy + 4) % 4
 
 
 def spread(index):
@@ -71,7 +70,8 @@
     x, c, z, y = place()
     for load in loads[:3]:
         load.wait()
-    expert = (table_v[...] + spread(x * 32 + c * 16 + z * 4 + y)) & spread(N - 1)
+    steps = jnp.where(c == 0, table_v[...], ((4 + 4 * 8 + 4 * 256) - (table_v[...] & ~64)) + (table_v[...] & 64))
+    expert = (steps + spread(x * 32 + c * 16 + z * 4 + y)) & spread(N - 1)
     asked = spread(ids_v[...])
     first = asked[0:1, :] == expert
     second = asked[1:2, :] == expert

time: 59.7 us -> 59.1 us (0.990)
  Pallas kernels: 58.8 us -> 58.2 us
    pallas_call x1, Pallas kernels: 58.8 us -> 58.2 us  [body(): pl.pallas_call(kernel, out_shape=pltpu.VMEM((rows, width), jnp.bfloat16),...]
where the time goes in v4:
time: 59.1 us; the launch traced here: 59 us
  Pallas kernels  58.2 us (98%)
  local copies, waits for them, and re-layouts  0.8 us (1%)
    pallas_call x1, Pallas kernels, body(): pl.pallas_call(kernel, out_shape=pltpu.VMEM((rows, width), jnp.bfloat16),...  58.2 us

profile of v4, /device:TPU:1, one launch (start us, length us, event | category | flops | bytes accessed | tf_op | source)
XLA Modules:
  0.0 59.0 jit_solution(13951852863691450648)
XLA Ops:
  0.0 58.2 %shard_map.73 = bf16[128,2048]{1,0:T(8,128)(2,1)S(1)} custom-call(bf16[128,2048]{1,0:T(8,128)(2,1)} %tokens.1, s32[2,128]{1,0:T(2,128)} %bitcast.2, s32[2,128]{1,0:T(2,128)} %bitcast.3, s32[512,128]{1,0:T(8,128)} %constant.2.clone.table, bf16[1,2048,1024]{2,1,0:T(8,128)(2,1)} %w_gate.1, bf16[1,2048,1024]{2,1,0:T(8,128)(2,1)} %w_up.1, ...), custom_call_target="tpu_custom_call" | custom-call | tf_op jit(solution)/shard_map/pallas_call | solution.py:163
  58.2 0.8 %copy.9 = bf16[128,2048]{1,0:T(8,128)(2,1)} copy(bf16[128,2048]{1,0:T(8,128)(2,1)S(1)} %shard_map.73) | data formatting | bytes 1048576

commit v5 on v4

--- a/solution.py
+++ b/solution.py
@@ -23,10 +23,12 @@
 
 OFFSETS = sorted(
     ((dx, dc, dz, dy) for dx in range(4) for dc in range(2) for dz in range(4) for dy in range(4) if dx + dc + dz + dy),
-    key=lambda offset: (turns(offset) == 3, -far(offset)),
-) + [(0, 0, 0, 0)]
+    key=lambda offset: -far(offset),
+)
+NEAR = [offset for offset in OFFSETS if turns(offset) < 3]
+EARLY = 32
+OFFSETS = NEAR[:EARLY] + [offset for offset in OFFSETS if turns(offset) == 3] + NEAR[EARLY:] + [(0, 0, 0, 0)]
 N = len(OFFSETS)
-NEAR = [offset for offset in OFFSETS[:-1] if turns(offset) < 3]
 COLUMN = [(0, 0, dz, 0) for dz in range(1, 4)]
 PER = N // CHUNKS
 ROWS = PER * CAP
@@ -92,7 +94,7 @@
             pl.semaphore_wait(barrier, len(NEAR))
             for offset in COLUMN:
                 pl.semaphore_signal(rest_sem, 1, device_id=device_at(offset, 1), device_id_type=MESH)
-        if (k + 1) * PER > len(NEAR) >= k * PER:
+        if (k + 1) * PER > EARLY >= k * PER:
             pl.semaphore_wait(rest_sem, len(COLUMN))
         for i in range(k * PER, min((k + 1) * PER, N - 1)):
             pltpu.make_async_remote_copy(

time: 59.1 us -> 59.1 us (level)
  no operation moved by 1% of the time
where the time goes in v5:
time: 59.1 us; the launch traced here: 59 us
  Pallas kernels  58.2 us (98%)
  local copies, waits for them, and re-layouts  0.8 us (1%)
    pallas_call x1, Pallas kernels, body(): pl.pallas_call(kernel, out_shape=pltpu.VMEM((rows, width), jnp.bfloat16),...  58.2 us

profile of v5, /device:TPU:1, one launch (start us, length us, event | category | flops | bytes accessed | tf_op | source)
XLA Modules:
  0.0 59.0 jit_solution(15187996113843889311)
XLA Ops:
  0.0 58.2 %shard_map.73 = bf16[128,2048]{1,0:T(8,128)(2,1)S(1)} custom-call(bf16[128,2048]{1,0:T(8,128)(2,1)} %tokens.1, s32[2,128]{1,0:T(2,128)} %bitcast.2, s32[2,128]{1,0:T(2,128)} %bitcast.3, s32[512,128]{1,0:T(8,128)} %constant.2.clone.table, bf16[1,2048,1024]{2,1,0:T(8,128)(2,1)} %w_gate.1, bf16[1,2048,1024]{2,1,0:T(8,128)(2,1)} %w_up.1, ...), custom_call_target="tpu_custom_call" | custom-call | tf_op jit(solution)/shard_map/pallas_call | solution.py:165
  58.2 0.8 %copy.9 = bf16[128,2048]{1,0:T(8,128)(2,1)} copy(bf16[128,2048]{1,0:T(8,128)(2,1)S(1)} %shard_map.73) | data formatting | bytes 1048576

commit v6 on v5

--- a/solution.py
+++ b/solution.py
@@ -29,6 +29,7 @@
 EARLY = 32
 OFFSETS = NEAR[:EARLY] + [offset for offset in OFFSETS if turns(offset) == 3] + NEAR[EARLY:] + [(0, 0, 0, 0)]
 N = len(OFFSETS)
+GREET = [offset for i, offset in enumerate(NEAR) if i < EARLY or offset[2] == 0 or offset[:2] + offset[3:] == (0, 0, 0)]
 COLUMN = [(0, 0, dz, 0) for dz in range(1, 4)]
 PER = N // CHUNKS
 ROWS = PER * CAP
@@ -57,8 +58,8 @@
     load_sem, send_sem, recv_sem, ret_sem, back_sem, own_sem, rest_sem,
 ):
     barrier = pltpu.get_barrier_semaphore()
-    for offset in NEAR:
-        pl.semaphore_signal(barrier, 1, device_id=device_at(offset, 1), device_id_type=MESH)
+    for offset in GREET:
+        pl.semaphore_signal(barrier, 1, device_id=device_at(offset, -1), device_id_type=MESH)
     loads = [
         pltpu.make_async_copy(src, dst, load_sem.at[i])
         for i, (src, dst) in enumerate((
@@ -91,7 +92,7 @@
         part = jnp.dot(pick[k * ROWS : (k + 1) * ROWS], tokens_v[...], preferred_element_type=jnp.float32)
         send[k * PER : (k + 1) * PER] = part.astype(jnp.bfloat16).reshape(PER, CAP, -1)
         if k == 0:
-            pl.semaphore_wait(barrier, len(NEAR))
+            pl.semaphore_wait(barrier, len(GREET))
             for offset in COLUMN:
                 pl.semaphore_signal(rest_sem, 1, device_id=device_at(offset, 1), device_id_type=MESH)
         if (k + 1) * PER > EARLY >= k * PER:

time: 59.1 us -> 59.1 us (level)
  no operation moved by 1% of the time
where the time goes in v6:
time: 59.1 us; the launch traced here: 59 us
  Pallas kernels  58.2 us (98%)
  local copies, waits for them, and re-layouts  0.8 us (1%)
    pallas_call x1, Pallas kernels, body(): pl.pallas_call(kernel, out_shape=pltpu.VMEM((rows, width), jnp.bfloat16),...  58.2 us

profile of v6, /device:TPU:1, one launch (start us, length us, event | category | flops | bytes accessed | tf_op | source)
XLA Modules:
  0.0 59.0 jit_solution(14244841366911899341)
XLA Ops:
  0.0 58.2 %shard_map.73 = bf16[128,2048]{1,0:T(8,128)(2,1)S(1)} custom-call(bf16[128,2048]{1,0:T(8,128)(2,1)} %tokens.1, s32[2,128]{1,0:T(2,128)} %bitcast.2, s32[2,128]{1,0:T(2,128)} %bitcast.3, s32[512,128]{1,0:T(8,128)} %constant.2.clone.table, bf16[1,2048,1024]{2,1,0:T(8,128)(2,1)} %w_gate.1, bf16[1,2048,1024]{2,1,0:T(8,128)(2,1)} %w_up.1, ...), custom_call_target="tpu_custom_call" | custom-call | tf_op jit(solution)/shard_map/pallas_call | solution.py:166
  58.2 0.8 %copy.9 = bf16[128,2048]{1,0:T(8,128)(2,1)} copy(bf16[128,2048]{1,0:T(8,128)(2,1)S(1)} %shard_map.73) | data formatting | bytes 1048576
